TPU v7x, 32 devices: a whole 2x2x4 slice. The times are simulated.
32 devices in a mesh: space: 8 (over z, y), pairs: 4 (over x, core).
Axes of the slice: x: 2, y: 2, z: 4, core: 2. Of those that a mesh axis runs over, the one named last changes fastest.
Arguments:
- positions: float32 [2048, 3, 512], P(('space', 'pairs')), may hold values from -3 to 25.2, as said below
- forces: float32 [2048, 3, 512], P(('space', 'pairs')), may hold values from -6 to 6
- pair_cells: int32 [2, 1536], P(None, ('space', 'pairs')), may hold values from 0 to 2047, as said below
- pair_count: int32 [32], P(('space', 'pairs')), may hold values from 6 to 48, as said below
Outputs:
- velocity: float32 [2048, 3, 512], P(('space', 'pairs'))
Inputs may be any that keep to these rules, and one draw needn't show every extreme that they name: `pair_cells`: device g holds cells [g * 64, (g + 1) * 64). Row 0 of its slot columns names one of its own cells. Row 1 names a cell other than row 0's; over the 48 slots of one device it names cells of each of the 12 devices of the device's region and of the two regions beside it exactly 4 times, the first and the last region counting as beside each other. Slots at or past a device's count hold pairs too but are not in its list. `pair_count`: in every region one device holds 48 live slots. `positions`: the cells of region r have their first coordinates within 1.2 of [3 r, 3 r + 3); the other two coordinates lie within -3 to 5.
All inputs are finite; a program needn't handle non-finite values.
Results may differ from a plain program's by a relative error of at most 0.0003.
Values sent between devices are 32-bit elements; how exact they have to be, the bound alone decides.
No kernel may reach another device: no remote copies, remote signals or barrier semaphores. Data moves between devices by JAX's collectives and lax.ppermute only.
A program may use at most 128 MiB of HBM per device.

v0:
```python
import math

import jax
import jax.numpy as jnp
from jax import lax
from jax.sharding import PartitionSpec as P

stokes_coef = 1.0 / (8.0 * math.pi)
eps_sq = 0.01
slab_width = 3.0


def extended(cells, sides, width):
    for axis, dim in sides:
        count = lax.axis_size(axis)
        head = lax.slice_in_dim(cells, 0, width, axis=dim)
        tail = lax.slice_in_dim(cells, cells.shape[dim] - width, cells.shape[dim], axis=dim)
        cells = jnp.concatenate(
            [
                lax.ppermute(tail, axis, [(i, (i + 1) % count) for i in range(count)]),
                cells,
                lax.ppermute(head, axis, [((i + 1) % count, i) for i in range(count)]),
            ],
            axis=dim,
        )
    return cells


def from_behind(value, axis, by):
    count = lax.axis_size(axis)
    return lax.ppermute(value, axis, [(i, (i + by) % count) for i in range(count)])


def pair_velocities(first_cell, second_cell, period):
    deltas = [
        first_cell[component][:, None] - second_cell[component][None, :] for component in range(3)
    ]
    half = 0.5 * period
    deltas[0] = jnp.where(
        deltas[0] > half,
        deltas[0] - period,
        jnp.where(deltas[0] < -half, deltas[0] + period, deltas[0]),
    )
    dist_sq = deltas[0] * deltas[0] + deltas[1] * deltas[1] + deltas[2] * deltas[2]
    inverse = lax.rsqrt(dist_sq + eps_sq)
    cubed = inverse * inverse * inverse * stokes_coef
    direct = (dist_sq + 2.0 * eps_sq) * cubed
    along_second = sum(
        (deltas[component] * second_cell[3 + component][None, :] for component in range(3))
    )
    along_first = sum(
        (deltas[component] * first_cell[3 + component][:, None] for component in range(3))
    )
    weight_second = cubed * along_second
    weight_first = cubed * along_first
    first_velocity = jnp.stack(
        [
            jnp.sum(
                direct * second_cell[3 + component][None, :] + weight_second * deltas[component],
                axis=1,
            )
            for component in range(3)
        ]
    )
    second_velocity = jnp.stack(
        [
            jnp.sum(
                direct * first_cell[3 + component][:, None] + weight_first * deltas[component],
                axis=0,
            )
            for component in range(3)
        ]
    )
    return (first_velocity, second_velocity)


def add_row(accum, index, value):
    current = lax.dynamic_slice_in_dim(accum, index, 1, 0)
    return lax.dynamic_update_slice_in_dim(accum, current + value[None], index, 0)


def body(positions, forces, pair_cells, pair_count):
    cell_data = jnp.concatenate([positions, forces], axis=1)
    cell_dev = cell_data.shape[0]
    points = cell_data.shape[2]
    n_pairs = lax.axis_size("pairs")
    n_space = lax.axis_size("space")
    region = cell_dev * n_pairs
    period = slab_width * n_space
    here = lax.axis_index("space")
    region_data = lax.all_gather(cell_data, "pairs", axis=0, tiled=True)
    nearby = extended(region_data, (("space", 0),), region)
    lower_end = jnp.int32(0)
    upper_end = pair_count[0]

    def locate(number):
        return lax.dynamic_slice_in_dim(pair_cells, number, 1, 1)[:, 0]

    def localize(cell):
        offset = (cell // region - here + 1 + n_space) % n_space
        return offset * region + cell % region

    def step(number, accum):
        cell_ids = localize(locate(number))
        first_id = cell_ids[0]
        second_id = cell_ids[1]
        first_cell = lax.dynamic_slice_in_dim(nearby, first_id, 1, 0)[0]
        second_cell = lax.dynamic_slice_in_dim(nearby, second_id, 1, 0)[0]
        first_velocity, second_velocity = pair_velocities(first_cell, second_cell, period)
        accum = add_row(accum, first_id, first_velocity)
        return add_row(accum, second_id, second_velocity)

    accum = lax.fori_loop(
        lower_end, upper_end, step, jnp.zeros((3 * region, 3, points), jnp.float32)
    )
    from_above = from_behind(accum[:region], "space", -1)
    from_below = from_behind(accum[2 * region :], "space", 1)
    region_total = accum[region : 2 * region] + from_above + from_below
    velocity = lax.psum_scatter(region_total, "pairs", scatter_dimension=0, tiled=True)
    return velocity


def solution(mesh):
    placed = (
        P(("space", "pairs"), None, None),
        P(("space", "pairs"), None, None),
        P(None, ("space", "pairs")),
        P(("space", "pairs")),
    )
    return jax.shard_map(
        body,
        mesh=mesh,
        in_specs=placed,
        out_specs=P(("space", "pairs"), None, None),
        check_vma=False,
    )
```

profile of v0, /device:TPU:0, one launch (start us, length us, event | category | flops | bytes accessed | tf_op | source)
XLA Modules:
  0.0 863.4 jit_solution(12616986580560340063)
XLA Ops:
  6.5 2.1 pad_maximum_fusion.1
  8.7 31.5 %all-gather.2.cloned.1.call-done = f32[256,6,512]{2,0,1:T(8,128)} async-done(((f32[64,6,512]{2,0,1:T(8,128)}), f32[256,6,512]{2,0,1:T(8,128)}) %all-gather.2.cloned.1.call-update) | async-done | bytes 3145744 | tf_op jit(solution)/shard_map/all_gather | solution.py:91
  40.2 4.2 collective-permute-start.1
  45.2 132.9 %collective-permute-done.1 = f32[256,6,512]{2,0,1:T(8,128)S(1)} collective-permute-done((f32[256,6,512]{2,0,1:T(8,128)}, f32[256,6,512]{2,0,1:T(8,128)S(1)}, u32[]{:S(2)}, u32[]{:S(2)}) %collective-permute-start.1) | collective-permute-done | bytes 3145760 | tf_op jit(solution)/shard_map/ppermute | solution.py:22
  178.1 8.3 pad_maximum_fusion
  186.4 13.9 %copy.17 = f32[768,6,512]{2,1,0:T(8,128)} copy(f32[768,6,512]{2,0,1:T(8,128)} %pad_maximum_fusion) | data formatting | bytes 18874368 | tf_op jit(solution)/shard_map/while | solution.py:113
  200.3 3.4 broadcast_in_dim.17
  203.7 183.7 %while.13 = (s32[]{:T(128)}, f32[768,3,512]{2,1,0:T(4,128)}, s32[]{:T(128)}, s32[2,48]{0,1:T(8,128)S(1)}, s32[]{:T(128)}, /*index=5*/f32[768,6,512]{2,1,0:T(8,12...) while((s32[]{:T(128)}, f32[768,3,512]{2,1,0:T(4,128)}, ...), condition=%wide.region_7.8_spmd, body=%wide.region_0.7_spmd.sunk | while | flops 14686292 | bytes 131459 | solution.py:113
  209.8 2.7 add_reduce_fusion.3
  221.3 2.7 add_reduce_fusion.3
  224.0 1.3 fusion.35
  225.3 1.3 fusion.36
  232.7 2.7 add_reduce_fusion.3
  244.2 2.7 add_reduce_fusion.3
  255.6 2.7 add_reduce_fusion.3
  267.1 2.7 add_reduce_fusion.3
  278.5 2.7 add_reduce_fusion.3
  289.9 2.7 add_reduce_fusion.3
  301.3 2.7 add_reduce_fusion.3
  312.7 2.7 add_reduce_fusion.3
  324.1 2.7 add_reduce_fusion.3
  335.6 2.7 add_reduce_fusion.3
  347.0 2.7 add_reduce_fusion.3
  358.4 2.7 add_reduce_fusion.3
  369.8 2.7 add_reduce_fusion.3
  381.3 2.7 add_reduce_fusion.3
  384.0 1.3 fusion.35
  387.4 4.3 copy.18
  392.2 48.1 %collective-permute-start.3 = (f32[256,3,512]{2,0,1:T(8,128)S(1)}, f32[256,3,512]{2,0,1:T(8,128)S(1)}, u32[]{:S(2)}, u32[]{:S(2)}) collective-permute-start(f32[256,3,512]{2,0,1:T(8,128)S(1)} %get-tuple-element.177), channel_id=1, source_target_pairs={{0,4},{4,8},{8,12},{12,16},{16,20},{20,24},{24,28},{28,0},{1,5},{5... | collective-permute-start | bytes 4718600 | tf_op jit(solution)/shard_map/ppermute | solution.py:31
  440.3 52.0 %collective-permute-done.2 = f32[256,3,512]{2,0,1:T(8,128)S(1)} collective-permute-done((f32[256,3,512]{2,0,1:T(8,128)S(1)}, f32[256,3,512]{2,0,1:T(8,128)S(1)}, u32[]{:S(2)}, u32[]{:S(2)}) %collective-permute-start.2) | collective-permute-done | bytes 1572896 | tf_op jit(solution)/shard_map/ppermute | solution.py:31
  492.3 1.7 fusion.26
  494.1 362.5 %reduce-scatter.2.cloned.1.call-done = f32[64,3,512]{2,0,1:T(8,128)} async-done(((f32[256,3,512]{2,0,1:T(8,128)}), f32[64,3,512]{2,0,1:T(8,128)}) %reduce-scatter.2.cloned.1.call-update) | async-done | bytes 393232 | tf_op jit(solution)/shard_map/reduce_scatter | solution.py:119
  (87 shorter events, 67.3 us)
Async XLA Ops:
  6.5 33.6 %all-gather.2.cloned.1.call-start = ((), (), s32[]{:S(2)}) async-start(), calls=%async_computation.1 | async-start | bytes 3932160 | tf_op jit(solution)/shard_map/all_gather | solution.py:91
  8.6 847.9 %reduce-scatter.2.cloned.1.call-start = ((), (), s32[]{:S(2)}) async-start(), calls=%async_computation.2 | async-start | bytes 1966080 | tf_op jit(solution)/shard_map/reduce_scatter | solution.py:119
  40.2 137.9 %collective-permute-start.1 = (f32[256,6,512]{2,0,1:T(8,128)}, f32[256,6,512]{2,0,1:T(8,128)S(1)}, u32[]{:S(2)}, u32[]{:S(2)}) collective-permute-start(f32[256,6,512]{2,0,1:T(8,128)} %all-gather.2.cloned.1.call-done), channel_id=1, source_target_pairs={{4,0},{8,4},{12,8},{16,12},{20,16},{24,20},{28,24},{0,28},{5,1},{9... | collective-permute-start | bytes 9437192 | tf_op jit(solution)/shard_map/ppermute | solution.py:22
  44.4 133.6 %collective-permute-start = (f32[256,6,512]{2,0,1:T(8,128)}, f32[256,6,512]{2,0,1:T(8,128)}, u32[]{:S(2)}, u32[]{:S(2)}) collective-permute-start(f32[256,6,512]{2,0,1:T(8,128)} %all-gather.2.cloned.1.call-done), channel_id=1, source_target_pairs={{0,4},{4,8},{8,12},{12,16},{16,20},{20,24},{24,28},{28,0},{1,5},{5... | collective-permute-start | bytes 9437192 | tf_op jit(solution)/shard_map/ppermute | solution.py:20
  392.1 100.2 %collective-permute-start.2 = (f32[256,3,512]{2,0,1:T(8,128)S(1)}, f32[256,3,512]{2,0,1:T(8,128)S(1)}, u32[]{:S(2)}, u32[]{:S(2)}) collective-permute-start(f32[256,3,512]{2,0,1:T(8,128)S(1)} %get-tuple-element.176), channel_id=1, source_target_pairs={{0,28},{4,0},{8,4},{12,8},{16,12},{20,16},{24,20},{28,24},{1,29},{... | collective-permute-start | bytes 4718600 | tf_op jit(solution)/shard_map/ppermute | solution.py:31
  392.2 100.1 %collective-permute-start.3 = (f32[256,3,512]{2,0,1:T(8,128)S(1)}, f32[256,3,512]{2,0,1:T(8,128)S(1)}, u32[]{:S(2)}, u32[]{:S(2)}) collective-permute-start(f32[256,3,512]{2,0,1:T(8,128)S(1)} %get-tuple-element.177), channel_id=1, source_target_pairs={{0,4},{4,8},{8,12},{12,16},{16,20},{20,24},{24,28},{28,0},{1,5},{5... | collective-permute-start | bytes 4718600 | tf_op jit(solution)/shard_map/ppermute | solution.py:31
Sparse Core Ops, SparseCore 0:
  8.9 31.2 all-gather.1
  494.2 362.3 reduce-scatter.1
where the time goes:
time: 869 us; the launch traced here: 863 us
  waiting for transfers between devices  579 us (67%)
  other arithmetic  97.7 us (11%)
  loops' own time  70.4 us (8%)
  starting transfers between devices  52.5 us (6%)
  local copies, waits for them, and re-layouts  50.5 us (6%)
  between operations  13.4 us (2%)
    reduce_scatter x1, waiting for transfers between devices, body(): lax.psum_scatter(region_total, 'pairs', scatter_dimension=0, tiled=True)  363 us
    ppermute x1, waiting for transfers between devices, extended(): lax.ppermute(head, axis, [((i + 1) % count, i) for i in range(count)])  133 us
    another operation x1, loops' own time, body(): lax.fori_loop(lower_end, upper_end, step, jnp.zeros((3 * region, 3, point...  70.4 us
    ppermute x2, waiting for transfers between devices, from_behind(): lax.ppermute(value, axis, [(i, (i + by) % count) for i in range(count)])  52 us
    ppermute x2, starting transfers between devices, from_behind(): lax.ppermute(value, axis, [(i, (i + by) % count) for i in range(count)])  48.2 us
    reduce_sum x16, other arithmetic, pair_velocities(): jnp.sum(direct * first_cell[3 + component][:, None] + weight_first * delt...  43.4 us
    dynamic_update_slice x32, other arithmetic, add_row(): lax.dynamic_update_slice_in_dim(accum, current + value[None], index, 0)  41.7 us
    all_gather x1, waiting for transfers between devices, body(): region_data = lax.all_gather(cell_data, 'pairs', axis=0, tiled=True)  31.5 us
  transfers between devices with their start and end apart: 6, of which 4 were waited for; matrix products, arithmetic and copies ran while one was open for 0% of the time, Pallas kernels for 0%

commit v1 on v0

v1 whole, which is shorter than its diff:
```python
import functools
import math

import jax
import jax.numpy as jnp
from jax import lax
from jax.experimental import pallas as pl
from jax.experimental.pallas import tpu as pltpu
from jax.sharding import PartitionSpec as P

stokes_coef = 1.0 / (8.0 * math.pi)
eps_sq = 0.01
slab_width = 3.0
across_middle = 1.0
LANES = 128
FEATURES = 16

f32 = jnp.float32
bf16 = jnp.bfloat16


def split(value, terms):
    parts = []
    for _ in range(terms - 1):
        part = value.astype(bf16).astype(f32)
        parts.append(part)
        value = value - part
    parts.append(value)
    return parts


def features(x, f):
    norm = jnp.sum(x * x, axis=0, keepdims=True)
    along = jnp.sum(x * f, axis=0, keepdims=True)
    rows = [f] + [x[k : k + 1] * f for k in range(3)] + [norm * f + x * along]
    rows.append(jnp.zeros_like(norm))
    stacked = jnp.concatenate(rows, axis=0)
    return jnp.concatenate([part.astype(bf16) for part in split(stacked, 3)], axis=0)


def combine(sums, y):
    force = sums[0:3]
    moment = [sums[3 + 3 * k : 6 + 3 * k] for k in range(3)]
    second = sums[12:15]
    norm = jnp.sum(y * y, axis=0, keepdims=True)
    trace = moment[0][0:1] + moment[1][1:2] + moment[2][2:3]
    along = jnp.sum(y * force, axis=0, keepdims=True) - trace
    turned = jnp.concatenate(
        [jnp.sum(y * moment[k], axis=0, keepdims=True) for k in range(3)], axis=0
    )
    mixed = y[0:1] * moment[0] + y[1:2] * moment[1] + y[2:3] * moment[2]
    velocity = (norm + 2.0 * eps_sq) * force + second - 2.0 * mixed + y * along - turned
    return velocity * stokes_coef


def gram_factors(x, y):
    one = jnp.ones((1, x.shape[1]), f32)
    none = jnp.zeros((3, x.shape[1]), f32)
    norm_x = jnp.sum(x * x, axis=0, keepdims=True)
    norm_y = jnp.sum(y * y, axis=0, keepdims=True) + eps_sq
    left = split(jnp.concatenate([x, norm_x, one, none], axis=0), 3)
    right = split(jnp.concatenate([-2.0 * y, one, norm_y, none], axis=0), 3)
    order = ((0, 0), (0, 1), (1, 0), (0, 2), (1, 1), (2, 0))
    return (
        jnp.concatenate([left[p] for p, _ in order], axis=0).astype(bf16),
        jnp.concatenate([right[q] for _, q in order], axis=0).astype(bf16),
    )


def dot(left, right, left_dim, right_dim):
    return lax.dot_general(
        left, right, (((left_dim,), (right_dim,)), ((), ())), preferred_element_type=f32
    )


def fold(high, low):
    return (
        high[0:FEATURES]
        + high[FEATURES : 2 * FEATURES]
        + high[2 * FEATURES :]
        + low[0:FEATURES]
        + low[FEATURES:]
    )


def pair_velocities(xa, fa, xb, fb):
    left, right = gram_factors(xa, xb)
    dist_sq = dot(left, right, 0, 0)
    inverse = lax.rsqrt(dist_sq)
    cubed = inverse * inverse * inverse
    high = cubed.astype(bf16)
    low = (cubed - high.astype(f32)).astype(bf16)
    feat_a = features(xa, fa)
    feat_b = features(xb, fb)
    two = 2 * FEATURES
    sums_b = fold(dot(feat_a, high, 1, 0), dot(feat_a[:two], low, 1, 0))
    sums_a = fold(dot(feat_b, high, 1, 1), dot(feat_b[:two], low, 1, 1))
    return combine(sums_a, xa), combine(sums_b, xb)


def pack_kernel(sizes, cells, count, pos, frc, *outs):
    n_space, n_pairs, share, cell_dev, tiles = sizes
    messages, table, slots, used = outs[:-3], outs[-3], outs[-2], outs[-1]
    n_slots = cells.shape[1]
    here = cells[0, 0] // cell_dev
    here_space = here // n_pairs
    here_pairs = lax.rem(here, n_pairs)

    def clear(i, _):
        used[i] = 0
        return 0

    lax.fori_loop(0, len(messages), clear, 0)

    def place(s, _):
        owner = cells[1, s] // cell_dev
        step = lax.rem(owner // n_pairs - here_space + 1 + n_space, n_space)
        turn = lax.rem(lax.rem(owner, n_pairs) - here_pairs + n_pairs, n_pairs)
        bucket = step * n_pairs + turn
        rank = used[bucket]
        used[bucket] = rank + 1
        slots[bucket * share + rank] = s
        return 0

    lax.fori_loop(0, n_slots, place, 0)
    lane = lax.broadcasted_iota(jnp.int32, (1, LANES), 1)
    for m, message in enumerate(messages):
        label = jnp.full((1, LANES), -1.0, f32)
        for k in range(share):
            s = slots[m * share + k]
            a = lax.rem(cells[0, s], cell_dev)
            live = s < count[0]
            b = jnp.where(live, lax.rem(cells[1, s], cell_dev), -1)
            table[m * share + k] = jnp.where(live, a, -1)
            label = jnp.where(lane == k, b.astype(f32), label)
            for c in range(6):
                source = pos if c < 3 else frc
                for t in range(tiles):
                    row = k * 6 * tiles + t * 6 + c
                    place_in = row_of(c % 3, a, t, cell_dev, tiles)
                    message[row : row + 1, :] = source[pl.ds(place_in, 1), :]
        last = share * 6 * tiles
        message[last : last + 1, :] = label


def pair_kernel(sizes, steps, cells, *refs):
    n_space, n_pairs, share, cell_dev, tiles = sizes
    n = len(steps)
    labels, messages = refs[:n], refs[n : 2 * n]
    pos, frc, acc_in, acc = refs[2 * n : 2 * n + 4]
    replies = refs[2 * n + 4 : 3 * n + 4]
    inbox, outbox, todo = refs[3 * n + 4 :]
    rows_in = share * 6 * tiles
    rows_out = share * 3 * tiles
    here_space = cells[0, 0] // (cell_dev * n_pairs)

    acc[...] = acc_in[...]
    number = jnp.int32(0)
    for m in range(n):
        inbox[m * rows_in : (m + 1) * rows_in, :] = messages[m][0:rows_in, :]
        for k in range(share):
            b = labels[m][0, k].astype(jnp.int32)
            todo[0, number] = m * share + k
            todo[1, number] = b
            todo[2, number] = steps[m]
            number = number + jnp.where(b >= 0, 1, 0)

    def one(i, _):
        slot = todo[0, i]
        b = todo[1, i]
        step = todo[2, i]
        from_space = lax.rem(here_space - step + n_space, n_space)
        half = 0.5 * slab_width * step.astype(f32)
        middle_a = slab_width * (from_space.astype(f32) + 0.5) + half
        middle_b = slab_width * (here_space.astype(f32) + 0.5) - half
        base = slot * (6 * tiles)
        block = jnp.concatenate(
            [inbox[pl.ds(base + 6 * t, 6), :] for t in range(tiles)], axis=1
        )
        axis = lax.broadcasted_iota(jnp.int32, (3, 1), 0)
        xa = block[0:3] - jnp.where(axis == 0, middle_a, across_middle)
        fa = block[3:6]
        where = [[row_of(c, b, t, cell_dev, tiles) for t in range(tiles)] for c in range(3)]
        xb, fb = (
            jnp.concatenate(
                [
                    jnp.concatenate([ref[pl.ds(row, 1), :] for row in rows], axis=1)
                    for rows in where
                ],
                axis=0,
            )
            for ref in (pos, frc)
        )
        xb = xb - jnp.where(axis == 0, middle_b, across_middle)
        vel_a, vel_b = pair_velocities(xa, fa, xb, fb)
        for c in range(3):
            for t in range(tiles):
                part = slice(t * LANES, (t + 1) * LANES)
                acc[pl.ds(where[c][t], 1), :] += vel_b[c : c + 1, part]
        base = slot * (3 * tiles)
        for t in range(tiles):
            outbox[pl.ds(base + 3 * t, 3), :] = vel_a[:, t * LANES : (t + 1) * LANES]
        return 0

    lax.fori_loop(0, number, one, 0)
    for m in range(n):
        replies[m][...] = outbox[m * rows_out : (m + 1) * rows_out, :]


def add_kernel(sizes, table, acc, *refs):
    _, _, share, cell_dev, tiles = sizes
    replies, out = refs[:-1], refs[-1]
    out[...] = acc[...]
    for m, reply in enumerate(replies):
        for k in range(share):
            a = table[m * share + k]
            live = a >= 0
            a = jnp.maximum(a, 0)
            for t in range(tiles):
                for c in range(3):
                    row = k * 3 * tiles + t * 3 + c
                    term = jnp.where(live, reply[row : row + 1, :], 0.0)
                    out[pl.ds(row_of(c, a, t, cell_dev, tiles), 1), :] += term


def flat_rows(cells):
    count, _, points = cells.shape
    value = jnp.transpose(cells, (1, 0, 2)).reshape(3, count // 8, 8, points // LANES, LANES)
    return jnp.transpose(value, (0, 1, 3, 2, 4)).reshape(-1, LANES)


def cell_rows(rows, count, points):
    value = rows.reshape(3, count // 8, points // LANES, 8, LANES)
    value = jnp.transpose(value, (0, 1, 3, 2, 4)).reshape(3, count, points)
    return jnp.transpose(value, (1, 0, 2))


def row_of(c, cell, t, cell_dev, tiles):
    return ((c * (cell_dev // 8) + cell // 8) * tiles + t) * 8 + lax.rem(cell, 8)


def body(positions, forces, pair_cells, pair_count):
    n_space = lax.axis_size("space")
    n_pairs = lax.axis_size("pairs")
    cell_dev, _, points = positions.shape
    n_slots = pair_cells.shape[1]
    n_messages = 3 * n_pairs
    share = n_slots // n_messages
    tiles = points // LANES
    sizes = (n_space, n_pairs, share, cell_dev, tiles)
    rows_in = share * 6 * tiles
    rows_out = share * 3 * tiles
    pos = flat_rows(positions)
    frc = flat_rows(forces)
    vmem = pl.BlockSpec(memory_space=pltpu.VMEM)
    smem = pl.BlockSpec(memory_space=pltpu.SMEM)
    limit = pltpu.CompilerParams(vmem_limit_bytes=48 * 1024 * 1024)

    message = jax.ShapeDtypeStruct((rows_in + 8, LANES), f32)
    reply = jax.ShapeDtypeStruct((rows_out, LANES), f32)
    total = jax.ShapeDtypeStruct((3 * cell_dev * tiles, LANES), f32)
    packed = pl.pallas_call(
        functools.partial(pack_kernel, sizes),
        out_shape=[message] * n_messages + [jax.ShapeDtypeStruct((n_slots,), jnp.int32)],
        in_specs=[smem, smem, vmem, vmem],
        out_specs=[vmem] * n_messages + [smem],
        scratch_shapes=[pltpu.SMEM((n_slots,), jnp.int32), pltpu.SMEM((n_messages,), jnp.int32)],
        compiler_params=limit,
        name="pack",
    )(pair_cells, pair_count, pos, frc)
    sent, table = packed[:-1], packed[-1]

    def moved(value, step, turn, back):
        if step == 0 and turn == 0:
            return value
        perm = []
        for i in range(n_space):
            for j in range(n_pairs):
                source = i * n_pairs + j
                target = (i + step) % n_space * n_pairs + (j + turn) % n_pairs
                perm.append((target, source) if back else (source, target))
        return lax.ppermute(value, ("space", "pairs"), perm)

    ways = [(step, turn) for step in (-1, 0, 1) for turn in range(n_pairs)]
    got = [moved(sent[m], *way, False) for m, way in enumerate(ways)]
    acc = jnp.zeros(total.shape, f32)
    replies = [None] * n_messages
    label = pl.BlockSpec((8, LANES), lambda i: (rows_in // 8, 0), memory_space=pltpu.SMEM)
    for wanted in (0, -1, 1):
        group = [m for m, way in enumerate(ways) if way[0] == wanted]
        n = len(group)
        arrived = [got[m] for m in group]
        results = pl.pallas_call(
            functools.partial(pair_kernel, sizes, [ways[m][0] for m in group]),
            out_shape=[total] + [reply] * n,
            grid=(1,),
            in_specs=[smem] + [label] * n + [vmem] * (n + 3),
            out_specs=[vmem] * (n + 1),
            scratch_shapes=[
                pltpu.VMEM((n * rows_in, LANES), f32),
                pltpu.VMEM((n * rows_out, LANES), f32),
                pltpu.SMEM((3, n * share + 1), jnp.int32),
            ],
            compiler_params=limit,
            cost_estimate=pl.CostEstimate(
                flops=4_000_000_000, bytes_accessed=2_000_000, transcendentals=2_000_000
            ),
            name="pairs",
        )(pair_cells, *arrived, *arrived, pos, frc, acc)
        acc = results[0]
        for m, value in zip(group, results[1:]):
            replies[m] = moved(value, *ways[m], True)

    velocity = pl.pallas_call(
        functools.partial(add_kernel, sizes),
        out_shape=total,
        in_specs=[smem] + [vmem] * (n_messages + 1),
        out_specs=vmem,
        compiler_params=limit,
        name="add",
    )(table, acc, *replies)
    return cell_rows(velocity, cell_dev, points)


def solution(mesh):
    placed = (
        P(("space", "pairs"), None, None),
        P(("space", "pairs"), None, None),
        P(None, ("space", "pairs")),
        P(("space", "pairs")),
    )
    return jax.shard_map(
        body,
        mesh=mesh,
        in_specs=placed,
        out_specs=P(("space", "pairs"), None, None),
        check_vma=False,
    )
```

time: 869 us -> 72.3 us (0.08)
  waiting for transfers between devices: 579 us -> 4.05 us
  other arithmetic: 97.7 us -> 0 us
  loops' own time: 70.4 us -> 0 us
  local copies, waits for them, and re-layouts: 50.5 us -> 2.69 us
  Pallas kernels: 0 us -> 30.7 us
  starting transfers between devices: 52.5 us -> 34.4 us
  between operations: 13.4 us -> 0.76 us
    reduce_scatter x1 -> x0, waiting for transfers between devices: 363 us -> none  [body(): lax.psum_scatter(region_total, 'pairs', scatter_dimension=0, tiled=True)]
    ppermute x4 -> x22, waiting for transfers between devices: 185 us -> 4.05 us  [moved(): return lax.ppermute(value, ('space', 'pairs'), perm)]
    another operation x1 -> x0, loops' own time: 70.4 us -> none  [body(): lax.fori_loop(lower_end, upper_end, step, jnp.zeros((3 * region, 3, point...]
    reduce_sum x16 -> x0, other arithmetic: 43.4 us -> none  [pair_velocities(): jnp.sum(direct * first_cell[3 + component][:, None] + weight_first * delt...]
    dynamic_update_slice x32 -> x0, other arithmetic: 41.7 us -> none  [add_row(): lax.dynamic_update_slice_in_dim(accum, current + value[None], index, 0)]
    all_gather x1 -> x0, waiting for transfers between devices: 31.5 us -> none  [body(): region_data = lax.all_gather(cell_data, 'pairs', axis=0, tiled=True)]
    pallas_call x0 -> x5, Pallas kernels: none -> 30.7 us  [the longest x3 25.3 us: body(): pl.pallas_call(functools.partial(pair_kernel, sizes, [ways[m][0] for m in...]
    slice x33 -> x0, local copies, waits for them, and re-layouts: 28.1 us -> none  [the longest x16 17.8 us: pair_velocities(): second_cell[3 + component][None, :]]
  transfers between devices with their start and end apart: 6 -> 22, of which waited for: 4 -> 3; matrix products, arithmetic and copies ran while one was open for 0% -> 0% of each run, Pallas kernels for 0% -> 21%
where the time goes in v1:
time: 72.3 us; the launch traced here: 72.6 us
  starting transfers between devices  34.4 us (48%)
  Pallas kernels  30.7 us (42%)
  waiting for transfers between devices  4.05 us (6%)
  local copies, waits for them, and re-layouts  2.69 us (4%)
  between operations  0.76 us (1%)
    ppermute x22, starting transfers between devices, moved(): return lax.ppermute(value, ('space', 'pairs'), perm)  34.4 us
    pallas_call x3, Pallas kernels, body(): pl.pallas_call(functools.partial(pair_kernel, sizes, [ways[m][0] for m in...  25.3 us
    ppermute x22, waiting for transfers between devices, moved(): return lax.ppermute(value, ('space', 'pairs'), perm)  4.05 us
    pallas_call x1, Pallas kernels, body(): pl.pallas_call(functools.partial(pack_kernel, sizes), out_shape=[message]...  3.68 us
    unnamed x6, local copies, waits for them, and re-layouts  2.66 us
    pallas_call x1, Pallas kernels, body(): pl.pallas_call(functools.partial(add_kernel, sizes), out_shape=total, in_...  1.72 us
  transfers between devices with their start and end apart: 22, of which 3 were waited for; matrix products, arithmetic and copies ran while one was open for 0% of the time, Pallas kernels for 21%

profile of v1, /device:TPU:0, one launch (start us, length us, event | category | flops | bytes accessed | tf_op | source)
XLA Modules:
  0.0 72.6 jit_solution(2214384037793907197)
XLA Ops:
  0.7 0.7 copy-done.2
  1.3 1.0 %copy-done = f32[64,3,512]{2,0,1:T(8,128)S(1)} copy-done((f32[64,3,512]{2,0,1:T(8,128)S(1)}, f32[64,3,512]{2,0,1:T(8,128)}, u32[]{:S(2)}) %copy-start) | copy-done | bytes 393240
  2.3 1.0 %copy-done.1 = f32[64,3,512]{2,0,1:T(8,128)S(1)} copy-done((f32[64,3,512]{2,0,1:T(8,128)S(1)}, f32[64,3,512]{2,0,1:T(8,128)}, u32[]{:S(2)}) %copy-start.1) | copy-done | bytes 393240
  3.3 3.7 %pack.1 = (f32[104,128]{1,0:T(8,128)S(1)}, f32[104,128]{1,0:T(8,128)S(1)}, f32[104,128]{1,0:T(8,128)S(1)}, f32[104,128]{1,0:T(8,128)S(1)}, f32[104,128]{1,0:T(8,...) custom-call(s32[2,48]{1,0:T(2,128)S(1)} %copy-done.2, ...), custom_call_target="tpu_custom_call" | custom-call | tf_op jit(solution)/shard_map/pack/pallas_call | solution.py:262
  7.0 0.5 collective-permute-start.8
  7.5 2.6 %collective-permute-start.9 = (f32[104,128]{1,0:T(8,128)S(1)}, f32[104,128]{1,0:T(8,128)S(1)}, u32[]{:S(2)}, u32[]{:S(2)}) collective-permute-start(f32[104,128]{1,0:T(8,128)S(1)} %get-tuple-element.44), channel_id=1, source_target_pairs={{0,2},{1,3},{2,0},{3,1},{4,6},{5,7},{6,4},{7,5},{8,10},{9,11},{10,... | collective-permute-start | bytes 159752 | tf_op jit(solution)/shard_map/ppermute | solution.py:282
  10.1 1.4 %collective-permute-start.10 = (f32[104,128]{1,0:T(8,128)S(1)}, f32[104,128]{1,0:T(8,128)S(1)}, u32[]{:S(2)}, u32[]{:S(2)}) collective-permute-start(f32[104,128]{1,0:T(8,128)S(1)} %get-tuple-element.45), channel_id=1, source_target_pairs={{0,3},{1,0},{2,1},{3,2},{4,7},{5,4},{6,5},{7,6},{8,11},{9,8},{10,9... | collective-permute-start | bytes 159752 | tf_op jit(solution)/shard_map/ppermute | solution.py:282
  11.5 1.5 %collective-permute-start = (f32[104,128]{1,0:T(8,128)S(1)}, f32[104,128]{1,0:T(8,128)S(1)}, u32[]{:S(2)}, u32[]{:S(2)}) collective-permute-start(f32[104,128]{1,0:T(8,128)S(1)} %get-tuple-element.34), channel_id=1, source_target_pairs={{0,4},{1,5},{2,6},{3,7},{4,8},{5,9},{6,10},{7,11},{8,12},{9,13},{1... | collective-permute-start | bytes 159752 | tf_op jit(solution)/shard_map/ppermute | solution.py:282
  13.0 3.2 %collective-permute-start.4 = (f32[104,128]{1,0:T(8,128)S(1)}, f32[104,128]{1,0:T(8,128)S(1)}, u32[]{:S(2)}, u32[]{:S(2)}) collective-permute-start(f32[104,128]{1,0:T(8,128)S(1)} %get-tuple-element.38), channel_id=1, source_target_pairs={{0,28},{1,29},{2,30},{3,31},{4,0},{5,1},{6,2},{7,3},{8,4},{9,5},{1... | collective-permute-start | bytes 159752 | tf_op jit(solution)/shard_map/ppermute | solution.py:282
  16.2 0.0 collective-permute-start.5
  16.2 0.0 collective-permute-done.9.refs_2_.refs_6_
  16.2 2.5 %collective-permute-start.6 = (f32[104,128]{1,0:T(8,128)S(1)}, f32[104,128]{1,0:T(8,128)S(1)}, u32[]{:S(2)}, u32[]{:S(2)}) collective-permute-start(f32[104,128]{1,0:T(8,128)S(1)} %get-tuple-element.40), channel_id=1, source_target_pairs={{0,30},{1,31},{2,28},{3,29},{4,2},{5,3},{6,0},{7,1},{8,6},{9,7},{1... | collective-permute-start | bytes 159752 | tf_op jit(solution)/shard_map/ppermute | solution.py:282
  18.7 0.0 collective-permute-done.10.refs_3_.refs_7_
  18.7 1.6 %collective-permute-start.7 = (f32[104,128]{1,0:T(8,128)S(1)}, f32[104,128]{1,0:T(8,128)S(1)}, u32[]{:S(2)}, u32[]{:S(2)}) collective-permute-start(f32[104,128]{1,0:T(8,128)S(1)} %get-tuple-element.41), channel_id=1, source_target_pairs={{0,31},{1,28},{2,29},{3,30},{4,3},{5,0},{6,1},{7,2},{8,7},{9,4},{1... | collective-permute-start | bytes 159752 | tf_op jit(solution)/shard_map/ppermute | solution.py:282
  20.3 8.1 %pairs.3 = (f32[768,128]{1,0:T(8,128)S(1)}, f32[48,128]{1,0:T(8,128)S(1)}, f32[48,128]{1,0:T(8,128)S(1)}, f32[48,128]{1,0:T(8,128)S(1)}, f32[48,128]{1,0:T(8,128)S(1)}) custom-call(s32[2,48]{1,0:T(2,128)S(1)} %copy-done.2, f32[104,128]{1,0:T(8,128)S(1)} %get-tuple-element.42.refs_0_.refs_4_, f32[104,128]{1,0:T(8,128)S(1)} %collective-permute-done.8.refs_1_.refs_5_, ...), custom_call_target="tpu_custom_call" | custom-call | flops 4000000000 | bytes 2000000 | tf_op jit(solution)/shard_map/pairs/pallas_call | solution.py:293
  28.5 1.1 %collective-permute-start.1 = (f32[104,128]{1,0:T(8,128)S(1)}, f32[104,128]{1,0:T(8,128)S(1)}, u32[]{:S(2)}, u32[]{:S(2)}) collective-permute-start(f32[104,128]{1,0:T(8,128)S(1)} %get-tuple-element.35), channel_id=1, source_target_pairs={{0,5},{1,6},{2,7},{3,4},{4,9},{5,10},{6,11},{7,8},{8,13},{9,14},{1... | collective-permute-start | bytes 159752 | tf_op jit(solution)/shard_map/ppermute | solution.py:282
  29.6 0.0 collective-permute-done.5.refs_1_.refs_5_
  29.6 2.7 %collective-permute-start.3 = (f32[104,128]{1,0:T(8,128)S(1)}, f32[104,128]{1,0:T(8,128)S(1)}, u32[]{:S(2)}, u32[]{:S(2)}) collective-permute-start(f32[104,128]{1,0:T(8,128)S(1)} %get-tuple-element.37), channel_id=1, source_target_pairs={{0,7},{1,4},{2,5},{3,6},{4,11},{5,8},{6,9},{7,10},{8,15},{9,12},{1... | collective-permute-start | bytes 159752 | tf_op jit(solution)/shard_map/ppermute | solution.py:282
  32.3 7.2 %pairs.4 = (f32[768,128]{1,0:T(8,128)S(1)}, f32[48,128]{1,0:T(8,128)S(1)}, f32[48,128]{1,0:T(8,128)S(1)}, f32[48,128]{1,0:T(8,128)S(1)}, f32[48,128]{1,0:T(8,128)S(1)}) custom-call(s32[2,48]{1,0:T(2,128)S(1)} %copy-done.2, f32[104,128]{1,0:T(8,128)S(1)} %collective-permute-done.4.refs_0_.refs_4_, f32[104,128]{1,0:T(8,128)S(1)} %collective-permute-done.5.refs_1_.refs_5_, ...), custom_call_target="tpu_custom_call" | custom-call | flops 4000000000 | bytes 2000000 | tf_op jit(solution)/shard_map/pairs/pallas_call | solution.py:293
  39.5 0.8 %collective-permute-done.3.refs_3_.refs_7_ = f32[104,128]{1,0:T(8,128)S(1)} collective-permute-done((f32[104,128]{1,0:T(8,128)S(1)}, f32[104,128]{1,0:T(8,128)S(1)}, u32[]{:S(2)}, u32[]{:S(2)}) %collective-permute-start.3) | collective-permute-done | bytes 53280 | tf_op jit(solution)/shard_map/ppermute | solution.py:282
  40.3 9.9 %pairs.5 = (f32[768,128]{1,0:T(8,128)S(1)}, f32[48,128]{1,0:T(8,128)S(1)}, f32[48,128]{1,0:T(8,128)S(1)}, f32[48,128]{1,0:T(8,128)S(1)}, f32[48,128]{1,0:T(8,128)S(1)}) custom-call(s32[2,48]{1,0:T(2,128)S(1)} %copy-done.2, f32[104,128]{1,0:T(8,128)S(1)} %collective-permute-done.refs_0_.refs_4_, f32[104,128]{1,0:T(8,128)S(1)} %collective-permute-done.1.refs_1_.refs_5_, ...), custom_call_target="tpu_custom_call" | custom-call | flops 4000000000 | bytes 2000000 | tf_op jit(solution)/shard_map/pairs/pallas_call | solution.py:293
  50.2 4.6 %collective-permute-start.18 = (f32[48,128]{1,0:T(8,128)S(1)}, f32[48,128]{1,0:T(8,128)S(1)}, u32[]{:S(2)}, u32[]{:S(2)}) collective-permute-start(f32[48,128]{1,0:T(8,128)S(1)} %get-tuple-element.57), channel_id=1, source_target_pairs={{4,0},{5,1},{6,2},{7,3},{8,4},{9,5},{10,6},{11,7},{12,8},{13,9},{1... | collective-permute-start | bytes 73736 | tf_op jit(solution)/shard_map/ppermute | solution.py:282
  54.9 1.2 %collective-permute-start.20 = (f32[48,128]{1,0:T(8,128)S(1)}, f32[48,128]{1,0:T(8,128)S(1)}, u32[]{:S(2)}, u32[]{:S(2)}) collective-permute-start(f32[48,128]{1,0:T(8,128)S(1)} %get-tuple-element.59), channel_id=1, source_target_pairs={{6,0},{7,1},{4,2},{5,3},{10,4},{11,5},{8,6},{9,7},{14,8},{15,9},{1... | collective-permute-start | bytes 73736 | tf_op jit(solution)/shard_map/ppermute | solution.py:282
  56.1 1.3 %collective-permute-start.21 = (f32[48,128]{1,0:T(8,128)S(1)}, f32[48,128]{1,0:T(8,128)S(1)}, u32[]{:S(2)}, u32[]{:S(2)}) collective-permute-start(f32[48,128]{1,0:T(8,128)S(1)} %get-tuple-element.60), channel_id=1, source_target_pairs={{7,0},{4,1},{5,2},{6,3},{11,4},{8,5},{9,6},{10,7},{15,8},{12,9},{1... | collective-permute-start | bytes 73736 | tf_op jit(solution)/shard_map/ppermute | solution.py:282
  57.4 2.3 %collective-permute-start.11 = (f32[48,128]{1,0:T(8,128)S(1)}, f32[48,128]{1,0:T(8,128)S(1)}, u32[]{:S(2)}, u32[]{:S(2)}) collective-permute-start(f32[48,128]{1,0:T(8,128)S(1)} %get-tuple-element.49), channel_id=1, source_target_pairs={{28,0},{29,1},{30,2},{31,3},{0,4},{1,5},{2,6},{3,7},{4,8},{5,9},{6... | collective-permute-start | bytes 73736 | tf_op jit(solution)/shard_map/ppermute | solution.py:282
  59.7 3.3 %collective-permute-start.12 = (f32[48,128]{1,0:T(8,128)S(1)}, f32[48,128]{1,0:T(8,128)S(1)}, u32[]{:S(2)}, u32[]{:S(2)}) collective-permute-start(f32[48,128]{1,0:T(8,128)S(1)} %get-tuple-element.50), channel_id=1, source_target_pairs={{29,0},{30,1},{31,2},{28,3},{1,4},{2,5},{3,6},{0,7},{5,8},{6,9},{7... | collective-permute-start | bytes 73736 | tf_op jit(solution)/shard_map/ppermute | solution.py:282
  63.0 1.4 %collective-permute-start.14 = (f32[48,128]{1,0:T(8,128)S(1)}, f32[48,128]{1,0:T(8,128)S(1)}, u32[]{:S(2)}, u32[]{:S(2)}) collective-permute-start(f32[48,128]{1,0:T(8,128)S(1)} %get-tuple-element.52), channel_id=1, source_target_pairs={{31,0},{28,1},{29,2},{30,3},{3,4},{0,5},{1,6},{2,7},{7,8},{4,9},{5... | collective-permute-start | bytes 73736 | tf_op jit(solution)/shard_map/ppermute | solution.py:282
  64.4 1.5 %collective-permute-start.15 = (f32[48,128]{1,0:T(8,128)S(1)}, f32[48,128]{1,0:T(8,128)S(1)}, u32[]{:S(2)}, u32[]{:S(2)}) collective-permute-start(f32[48,128]{1,0:T(8,128)S(1)} %get-tuple-element.54), channel_id=1, source_target_pairs={{1,0},{2,1},{3,2},{0,3},{5,4},{6,5},{7,6},{4,7},{9,8},{10,9},{11,1... | collective-permute-start | bytes 73736 | tf_op jit(solution)/shard_map/ppermute | solution.py:282
  65.9 1.7 %collective-permute-start.16 = (f32[48,128]{1,0:T(8,128)S(1)}, f32[48,128]{1,0:T(8,128)S(1)}, u32[]{:S(2)}, u32[]{:S(2)}) collective-permute-start(f32[48,128]{1,0:T(8,128)S(1)} %get-tuple-element.55), channel_id=1, source_target_pairs={{2,0},{3,1},{0,2},{1,3},{6,4},{7,5},{4,6},{5,7},{10,8},{11,9},{8,1... | collective-permute-start | bytes 73736 | tf_op jit(solution)/shard_map/ppermute | solution.py:282
  67.6 2.8 %collective-permute-done.13.refs_2_ = f32[48,128]{1,0:T(8,128)S(1)} collective-permute-done((f32[48,128]{1,0:T(8,128)S(1)}, f32[48,128]{1,0:T(8,128)S(1)}, u32[]{:S(2)}, u32[]{:S(2)}) %collective-permute-start.13) | collective-permute-done | bytes 24608 | tf_op jit(solution)/shard_map/ppermute | solution.py:282
  70.4 0.4 collective-permute-done.17.refs_7_
  70.8 1.7 %add.1 = f32[768,128]{1,0:T(8,128)} custom-call(s32[48]{0:T(128)S(1)} %get-tuple-element.33.table, f32[768,128]{1,0:T(8,128)S(1)} %get-tuple-element.48.acc, f32[48,128]{1,0:T(8,128)S(1)} %collective-permute-done.11.refs_0_, f32[48,128]{1,0:T(8,128)S(1)} %collective-permute-done.12.refs_1_, f32[48,128]{1,0:T(8,128)S(1)} %collective-permute-done.13.refs_2_, ...), custom_call_target="tpu_custom_call" | custom-call | tf_op jit(solution)/shard_map/add/pallas_call | solution.py:314
  (24 shorter events, 0.1 us)
Async XLA Ops:
  0.7 0.7 copy-start.2
  1.3 1.0 %copy-start = (f32[64,3,512]{2,0,1:T(8,128)S(1)}, f32[64,3,512]{2,0,1:T(8,128)}, u32[]{:S(2)}) copy-start(f32[64,3,512]{2,0,1:T(8,128)} %param.4) | copy-start | bytes 1179652
  2.3 1.0 %copy-start.1 = (f32[64,3,512]{2,0,1:T(8,128)S(1)}, f32[64,3,512]{2,0,1:T(8,128)}, u32[]{:S(2)}) copy-start(f32[64,3,512]{2,0,1:T(8,128)} %param.5) | copy-start | bytes 1179652
  7.0 9.2 %collective-permute-start.8 = (f32[104,128]{1,0:T(8,128)S(1)}, f32[104,128]{1,0:T(8,128)S(1)}, u32[]{:S(2)}, u32[]{:S(2)}) collective-permute-start(f32[104,128]{1,0:T(8,128)S(1)} %get-tuple-element.43), channel_id=1, source_target_pairs={{0,1},{1,2},{2,3},{3,0},{4,5},{5,6},{6,7},{7,4},{8,9},{9,10},{10,1... | collective-permute-start | bytes 159752 | tf_op jit(solution)/shard_map/ppermute | solution.py:282
  7.5 8.7 %collective-permute-start.9 = (f32[104,128]{1,0:T(8,128)S(1)}, f32[104,128]{1,0:T(8,128)S(1)}, u32[]{:S(2)}, u32[]{:S(2)}) collective-permute-start(f32[104,128]{1,0:T(8,128)S(1)} %get-tuple-element.44), channel_id=1, source_target_pairs={{0,2},{1,3},{2,0},{3,1},{4,6},{5,7},{6,4},{7,5},{8,10},{9,11},{10,... | collective-permute-start | bytes 159752 | tf_op jit(solution)/shard_map/ppermute | solution.py:282
  10.1 8.6 %collective-permute-start.10 = (f32[104,128]{1,0:T(8,128)S(1)}, f32[104,128]{1,0:T(8,128)S(1)}, u32[]{:S(2)}, u32[]{:S(2)}) collective-permute-start(f32[104,128]{1,0:T(8,128)S(1)} %get-tuple-element.45), channel_id=1, source_target_pairs={{0,3},{1,0},{2,1},{3,2},{4,7},{5,4},{6,5},{7,6},{8,11},{9,8},{10,9... | collective-permute-start | bytes 159752 | tf_op jit(solution)/shard_map/ppermute | solution.py:282
  11.5 28.0 %collective-permute-start = (f32[104,128]{1,0:T(8,128)S(1)}, f32[104,128]{1,0:T(8,128)S(1)}, u32[]{:S(2)}, u32[]{:S(2)}) collective-permute-start(f32[104,128]{1,0:T(8,128)S(1)} %get-tuple-element.34), channel_id=1, source_target_pairs={{0,4},{1,5},{2,6},{3,7},{4,8},{5,9},{6,10},{7,11},{8,12},{9,13},{1... | collective-permute-start | bytes 159752 | tf_op jit(solution)/shard_map/ppermute | solution.py:282
  13.0 15.5 %collective-permute-start.4 = (f32[104,128]{1,0:T(8,128)S(1)}, f32[104,128]{1,0:T(8,128)S(1)}, u32[]{:S(2)}, u32[]{:S(2)}) collective-permute-start(f32[104,128]{1,0:T(8,128)S(1)} %get-tuple-element.38), channel_id=1, source_target_pairs={{0,28},{1,29},{2,30},{3,31},{4,0},{5,1},{6,2},{7,3},{8,4},{9,5},{1... | collective-permute-start | bytes 159752 | tf_op jit(solution)/shard_map/ppermute | solution.py:282
  16.2 13.4 %collective-permute-start.5 = (f32[104,128]{1,0:T(8,128)S(1)}, f32[104,128]{1,0:T(8,128)S(1)}, u32[]{:S(2)}, u32[]{:S(2)}) collective-permute-start(f32[104,128]{1,0:T(8,128)S(1)} %get-tuple-element.39), channel_id=1, source_target_pairs={{0,29},{1,30},{2,31},{3,28},{4,1},{5,2},{6,3},{7,0},{8,5},{9,6},{1... | collective-permute-start | bytes 159752 | tf_op jit(solution)/shard_map/ppermute | solution.py:282
  16.2 13.4 %collective-permute-start.6 = (f32[104,128]{1,0:T(8,128)S(1)}, f32[104,128]{1,0:T(8,128)S(1)}, u32[]{:S(2)}, u32[]{:S(2)}) collective-permute-start(f32[104,128]{1,0:T(8,128)S(1)} %get-tuple-element.40), channel_id=1, source_target_pairs={{0,30},{1,31},{2,28},{3,29},{4,2},{5,3},{6,0},{7,1},{8,6},{9,7},{1... | collective-permute-start | bytes 159752 | tf_op jit(solution)/shard_map/ppermute | solution.py:282
  18.7 13.6 %collective-permute-start.7 = (f32[104,128]{1,0:T(8,128)S(1)}, f32[104,128]{1,0:T(8,128)S(1)}, u32[]{:S(2)}, u32[]{:S(2)}) collective-permute-start(f32[104,128]{1,0:T(8,128)S(1)} %get-tuple-element.41), channel_id=1, source_target_pairs={{0,31},{1,28},{2,29},{3,30},{4,3},{5,0},{6,1},{7,2},{8,7},{9,4},{1... | collective-permute-start | bytes 159752 | tf_op jit(solution)/shard_map/ppermute | solution.py:282
  28.5 11.0 %collective-permute-start.1 = (f32[104,128]{1,0:T(8,128)S(1)}, f32[104,128]{1,0:T(8,128)S(1)}, u32[]{:S(2)}, u32[]{:S(2)}) collective-permute-start(f32[104,128]{1,0:T(8,128)S(1)} %get-tuple-element.35), channel_id=1, source_target_pairs={{0,5},{1,6},{2,7},{3,4},{4,9},{5,10},{6,11},{7,8},{8,13},{9,14},{1... | collective-permute-start | bytes 159752 | tf_op jit(solution)/shard_map/ppermute | solution.py:282
  29.6 9.9 %collective-permute-start.2 = (f32[104,128]{1,0:T(8,128)S(1)}, f32[104,128]{1,0:T(8,128)S(1)}, u32[]{:S(2)}, u32[]{:S(2)}) collective-permute-start(f32[104,128]{1,0:T(8,128)S(1)} %get-tuple-element.36), channel_id=1, source_target_pairs={{0,6},{1,7},{2,4},{3,5},{4,10},{5,11},{6,8},{7,9},{8,14},{9,15},{1... | collective-permute-start | bytes 159752 | tf_op jit(solution)/shard_map/ppermute | solution.py:282
  29.6 10.7 %collective-permute-start.3 = (f32[104,128]{1,0:T(8,128)S(1)}, f32[104,128]{1,0:T(8,128)S(1)}, u32[]{:S(2)}, u32[]{:S(2)}) collective-permute-start(f32[104,128]{1,0:T(8,128)S(1)} %get-tuple-element.37), channel_id=1, source_target_pairs={{0,7},{1,4},{2,5},{3,6},{4,11},{5,8},{6,9},{7,10},{8,15},{9,12},{1... | collective-permute-start | bytes 159752 | tf_op jit(solution)/shard_map/ppermute | solution.py:282
  50.2 9.5 %collective-permute-start.18 = (f32[48,128]{1,0:T(8,128)S(1)}, f32[48,128]{1,0:T(8,128)S(1)}, u32[]{:S(2)}, u32[]{:S(2)}) collective-permute-start(f32[48,128]{1,0:T(8,128)S(1)} %get-tuple-element.57), channel_id=1, source_target_pairs={{4,0},{5,1},{6,2},{7,3},{8,4},{9,5},{10,6},{11,7},{12,8},{13,9},{1... | collective-permute-start | bytes 73736 | tf_op jit(solution)/shard_map/ppermute | solution.py:282
  54.9 8.1 %collective-permute-start.19 = (f32[48,128]{1,0:T(8,128)S(1)}, f32[48,128]{1,0:T(8,128)S(1)}, u32[]{:S(2)}, u32[]{:S(2)}) collective-permute-start(f32[48,128]{1,0:T(8,128)S(1)} %get-tuple-element.58), channel_id=1, source_target_pairs={{5,0},{6,1},{7,2},{4,3},{9,4},{10,5},{11,6},{8,7},{13,8},{14,9},{1... | collective-permute-start | bytes 73736 | tf_op jit(solution)/shard_map/ppermute | solution.py:282
  54.9 8.1 %collective-permute-start.20 = (f32[48,128]{1,0:T(8,128)S(1)}, f32[48,128]{1,0:T(8,128)S(1)}, u32[]{:S(2)}, u32[]{:S(2)}) collective-permute-start(f32[48,128]{1,0:T(8,128)S(1)} %get-tuple-element.59), channel_id=1, source_target_pairs={{6,0},{7,1},{4,2},{5,3},{10,4},{11,5},{8,6},{9,7},{14,8},{15,9},{1... | collective-permute-start | bytes 73736 | tf_op jit(solution)/shard_map/ppermute | solution.py:282
  56.1 8.4 %collective-permute-start.21 = (f32[48,128]{1,0:T(8,128)S(1)}, f32[48,128]{1,0:T(8,128)S(1)}, u32[]{:S(2)}, u32[]{:S(2)}) collective-permute-start(f32[48,128]{1,0:T(8,128)S(1)} %get-tuple-element.60), channel_id=1, source_target_pairs={{7,0},{4,1},{5,2},{6,3},{11,4},{8,5},{9,6},{10,7},{15,8},{12,9},{1... | collective-permute-start | bytes 73736 | tf_op jit(solution)/shard_map/ppermute | solution.py:282
  57.4 8.5 %collective-permute-start.11 = (f32[48,128]{1,0:T(8,128)S(1)}, f32[48,128]{1,0:T(8,128)S(1)}, u32[]{:S(2)}, u32[]{:S(2)}) collective-permute-start(f32[48,128]{1,0:T(8,128)S(1)} %get-tuple-element.49), channel_id=1, source_target_pairs={{28,0},{29,1},{30,2},{31,3},{0,4},{1,5},{2,6},{3,7},{4,8},{5,9},{6... | collective-permute-start | bytes 73736 | tf_op jit(solution)/shard_map/ppermute | solution.py:282
  59.7 7.9 %collective-permute-start.12 = (f32[48,128]{1,0:T(8,128)S(1)}, f32[48,128]{1,0:T(8,128)S(1)}, u32[]{:S(2)}, u32[]{:S(2)}) collective-permute-start(f32[48,128]{1,0:T(8,128)S(1)} %get-tuple-element.50), channel_id=1, source_target_pairs={{29,0},{30,1},{31,2},{28,3},{1,4},{2,5},{3,6},{0,7},{5,8},{6,9},{7... | collective-permute-start | bytes 73736 | tf_op jit(solution)/shard_map/ppermute | solution.py:282
  63.0 7.4 %collective-permute-start.13 = (f32[48,128]{1,0:T(8,128)S(1)}, f32[48,128]{1,0:T(8,128)S(1)}, u32[]{:S(2)}, u32[]{:S(2)}) collective-permute-start(f32[48,128]{1,0:T(8,128)S(1)} %get-tuple-element.51), channel_id=1, source_target_pairs={{30,0},{31,1},{28,2},{29,3},{2,4},{3,5},{0,6},{1,7},{6,8},{7,9},{4... | collective-permute-start | bytes 73736 | tf_op jit(solution)/shard_map/ppermute | solution.py:282
  63.0 7.4 %collective-permute-start.14 = (f32[48,128]{1,0:T(8,128)S(1)}, f32[48,128]{1,0:T(8,128)S(1)}, u32[]{:S(2)}, u32[]{:S(2)}) collective-permute-start(f32[48,128]{1,0:T(8,128)S(1)} %get-tuple-element.52), channel_id=1, source_target_pairs={{31,0},{28,1},{29,2},{30,3},{3,4},{0,5},{1,6},{2,7},{7,8},{4,9},{5... | collective-permute-start | bytes 73736 | tf_op jit(solution)/shard_map/ppermute | solution.py:282
  64.4 6.0 %collective-permute-start.15 = (f32[48,128]{1,0:T(8,128)S(1)}, f32[48,128]{1,0:T(8,128)S(1)}, u32[]{:S(2)}, u32[]{:S(2)}) collective-permute-start(f32[48,128]{1,0:T(8,128)S(1)} %get-tuple-element.54), channel_id=1, source_target_pairs={{1,0},{2,1},{3,2},{0,3},{5,4},{6,5},{7,6},{4,7},{9,8},{10,9},{11,1... | collective-permute-start | bytes 73736 | tf_op jit(solution)/shard_map/ppermute | solution.py:282
  65.9 4.5 %collective-permute-start.16 = (f32[48,128]{1,0:T(8,128)S(1)}, f32[48,128]{1,0:T(8,128)S(1)}, u32[]{:S(2)}, u32[]{:S(2)}) collective-permute-start(f32[48,128]{1,0:T(8,128)S(1)} %get-tuple-element.55), channel_id=1, source_target_pairs={{2,0},{3,1},{0,2},{1,3},{6,4},{7,5},{4,6},{5,7},{10,8},{11,9},{8,1... | collective-permute-start | bytes 73736 | tf_op jit(solution)/shard_map/ppermute | solution.py:282
  67.6 3.3 %collective-permute-start.17 = (f32[48,128]{1,0:T(8,128)S(1)}, f32[48,128]{1,0:T(8,128)S(1)}, u32[]{:S(2)}, u32[]{:S(2)}) collective-permute-start(f32[48,128]{1,0:T(8,128)S(1)} %get-tuple-element.56), channel_id=1, source_target_pairs={{3,0},{0,1},{1,2},{2,3},{7,4},{4,5},{5,6},{6,7},{11,8},{8,9},{9,10... | collective-permute-start | bytes 73736 | tf_op jit(solution)/shard_map/ppermute | solution.py:282
